TPU v7x, 32 devices: a whole 2x2x4 slice. The times are simulated.
32 devices in a mesh: seq: 8 (over z, x), head: 4 (over y, core).
Axes of the slice: x: 2, y: 2, z: 4, core: 2. Of those that a mesh axis runs over, the one named last changes fastest.
Arguments:
- inputs: bfloat16 [8192, 4096], P('seq', 'head'), as said below
- gate_input: bfloat16 [8192, 4096], P('seq', 'head'), may hold values from -6 to 6
- log_decay: float32 [8192, 64], P('seq', 'head'), as said below
- b_matrix: bfloat16 [8192, 4, 128], P('seq', 'head'), may hold values from -6 to 6
- c_matrix: bfloat16 [8192, 4, 128], P('seq', 'head'), may hold values from -1.25 to 1.25
- norm_gain: float32 [4096], P('head'), may hold values from 0.1 to 1.9
- cotangent: bfloat16 [8192, 4096], P('seq', 'head'), may hold values from -6 to 6
Outputs:
- normed: bfloat16 [8192, 4096], P('seq', 'head')
- grad_inputs: bfloat16 [8192, 4096], P('seq', 'head')
- grad_gate: bfloat16 [8192, 4096], P('seq', 'head')
- grad_decay: float32 [8192, 64], P('seq', 'head')
- grad_b_matrix: float32 [8192, 4, 128], P('seq', 'head')
- grad_c_matrix: float32 [8192, 4, 128], P('seq', 'head')
Inputs may be any that keep to these rules, and one draw needn't show every extreme that they name: `log_decay`: every entry is strictly negative. `inputs`: real-valued and finite.
All inputs are finite; a program needn't handle non-finite values.
Results may differ from a plain program's by a relative error of at most 0.003.
Values sent between devices are 32-bit elements; how exact they have to be, the bound alone decides.
A program may use at most 192 MiB of HBM per device.

v0:
```python
import functools

import jax
import jax.numpy as jnp
from jax import lax
from jax.experimental import pallas as pl
from jax.experimental.pallas import tpu as pltpu
from jax.sharding import PartitionSpec as P

SPAN = 128
EPSILON = 1e-05
F32 = jnp.float32
BF16 = jnp.bfloat16
VMEM_BYTES = 48 * 1024 * 1024


def split2(v):
    high = v.astype(BF16)
    return high, (v - high.astype(F32)).astype(BF16)


def split3(v):
    high, rest = v.astype(BF16), v
    rest = rest - high.astype(F32)
    mid = rest.astype(BF16)
    return high, mid, (rest - mid.astype(F32)).astype(BF16)


def dot(a, b, ca=1, cb=0):
    return lax.dot_general(a, b, (((ca,), (cb,)), ((), ())), preferred_element_type=F32)


def iotas(rows, cols):
    return (
        lax.broadcasted_iota(jnp.int32, (rows, cols), 0),
        lax.broadcasted_iota(jnp.int32, (rows, cols), 1),
    )


def spread_matrix(heads, width):
    row, col = iotas(heads, width)
    size = width // heads
    return jnp.where((col >= row * size) & (col < (row + 1) * size), 1.0, 0.0).astype(BF16)


def gather_matrix(heads, width):
    row, col = iotas(width, heads)
    size = width // heads
    return jnp.where((row >= col * size) & (row < (col + 1) * size), 1.0, 0.0).astype(BF16)


def spread(v, width):
    matrix = spread_matrix(v.shape[1], width)
    return sum(dot(p, matrix) for p in split3(v))


def head_sums(v, heads):
    matrix = gather_matrix(heads, v.shape[1])
    return sum(dot(p, matrix) for p in split3(v))


def running_sums(a):
    row, col = iotas(SPAN, SPAN)
    lower = jnp.where(row >= col, 1.0, 0.0).astype(BF16)
    return dot(jnp.concatenate([lower] * 3, 1), jnp.concatenate(split3(a), 0))


def state_terms(scaled, matrix_half):
    return dot(
        jnp.concatenate([matrix_half] * 2, 0), jnp.concatenate(split2(scaled), 0), 0, 0
    )


def read_state(matrix_half, state_parts):
    return dot(jnp.concatenate([matrix_half] * 2, 1), jnp.concatenate(state_parts, 0))


def local_state_kernel(x_ref, a_ref, b_ref, out_ref):
    width = x_ref.shape[1]
    size = b_ref.shape[1]

    @pl.when(pl.program_id(0) == 0)
    def _():
        out_ref[...] = jnp.zeros_like(out_ref)

    running = running_sums(a_ref[...])
    end = running[SPAN - 1 :, :]
    scaled = x_ref[...].astype(F32) * spread(jnp.exp(end - running), width)
    end_wide = spread(jnp.broadcast_to(end, (8, end.shape[1])), width)
    out_ref[:size, :] = out_ref[:size, :] * jnp.exp(end_wide[:1, :]) + state_terms(
        scaled, b_ref[...]
    )
    out_ref[size:, :] += end_wide


def pair_columns(pair_x, first):
    col = lax.broadcasted_iota(jnp.int32, pair_x.shape, 1)
    half = pair_x.shape[1] // 2
    keep = col < half if first else col >= half
    return jnp.where(keep, pair_x, jnp.zeros_like(pair_x))


def decays_of(running, running_rows, head, causal):
    gaps = running[:, head : head + 1] - running_rows[head : head + 1, :]
    return jnp.exp(jnp.where(causal, gaps, -1e30))


def rows_of(running):
    heads = running.shape[1]
    padded = jnp.concatenate([running, jnp.zeros((SPAN, SPAN - heads), F32)], 1)
    return jnp.transpose(padded)[:heads, :]


def diagonal_kernel(x_ref, a_ref, b_ref, c_ref, y_ref):
    heads = a_ref.shape[1]
    size = x_ref.shape[1] // heads
    running = running_sums(a_ref[...])
    running_rows = rows_of(running)
    row, col = iotas(SPAN, SPAN)
    causal = row >= col
    scores = dot(c_ref[...], b_ref[...], 1, 1)
    for pair in range(heads // 2):
        cols = slice(pair * 2 * size, (pair + 1) * 2 * size)
        x_pair = x_ref[:, cols]
        left, right = [], []
        for which in range(2):
            weighted = decays_of(running, running_rows, 2 * pair + which, causal) * scores
            left += list(split2(weighted))
            right += [pair_columns(x_pair, which == 0)] * 2
        y_ref[:, cols] = dot(jnp.concatenate(left, 1), jnp.concatenate(right, 0))


def carried(gathered_ref, size, reverse):
    count = gathered_ref.shape[0]
    place = lax.axis_index("seq")
    state = jnp.zeros((size, gathered_ref.shape[2]), F32)
    for hop in range(count - 1):
        source = count - 1 - hop if reverse else hop
        use = source > place if reverse else source < place
        later = jnp.exp(gathered_ref[source, size : size + 1, :]) * state
        state = jnp.where(use, later + gathered_ref[source, :size, :], state)
    return state


def silu_parts(gate_ref):
    gate = gate_ref[...].astype(F32)
    sigmoid = 1.0 / (1.0 + jnp.exp(-gate))
    return gate, sigmoid


def row_total(v):
    folded = v[:, :SPAN]
    for start in range(SPAN, v.shape[1], SPAN):
        folded = folded + v[:, start : start + SPAN]
    return jnp.sum(jnp.transpose(folded), axis=0, keepdims=True)


def forward_kernel(
    diag_ref, x_ref, a_ref, b_ref, c_ref, gate_ref, cot_ref, gain_ref, gathered_ref,
    y_ref, state_ref, sums_ref, carry,
):
    width = x_ref.shape[1]
    size = b_ref.shape[1]

    @pl.when(pl.program_id(0) == 0)
    def _():
        carry[...] = carried(gathered_ref, size, False)

    running = running_sums(a_ref[...])
    end = running[SPAN - 1 :, :]
    state = carry[...]
    state_ref[...] = state
    out = diag_ref[...] + spread(jnp.exp(running), width) * read_state(
        c_ref[...], split2(state)
    )
    y_ref[...] = out
    to_end = spread(jnp.exp(end - running), width)
    scaled = x_ref[...].astype(F32) * to_end
    end_wide = spread(jnp.broadcast_to(jnp.exp(end), (8, end.shape[1])), width)
    carry[...] = state * end_wide[:1, :] + state_terms(scaled, b_ref[...])
    gate, sigmoid = silu_parts(gate_ref)
    gated = out * (gate * sigmoid)
    scaled_cot = gain_ref[...] * cot_ref[...].astype(F32)
    squares = row_total(gated * gated)
    products = row_total(gated * scaled_cot)
    which = lax.broadcasted_iota(jnp.int32, sums_ref.shape, 0)
    sums_ref[...] = jnp.where(which == 0, squares, jnp.where(which == 1, products, 0.0))


def norm_kernel(
    full_width, y_ref, a_ref, c_ref, gate_ref, cot_ref, gain_ref, sums_ref,
    normed_ref, grad_gate_ref, up_ref, leaving_ref, before,
):
    width = y_ref.shape[1]

    @pl.when(pl.program_id(0) == 0)
    def _():
        leaving_ref[...] = jnp.zeros_like(leaving_ref)
        before[...] = jnp.zeros_like(before)

    sums = sums_ref[...]
    columns = jnp.transpose(
        jnp.concatenate([sums, jnp.zeros((SPAN - sums.shape[0], SPAN), F32)], 0)
    )
    squares, products = columns[:, 0:1], columns[:, 1:2]
    inverse_rms = lax.rsqrt(squares / full_width + EPSILON)
    factor = inverse_rms * inverse_rms * inverse_rms * products / full_width
    out = y_ref[...]
    gate, sigmoid = silu_parts(gate_ref)
    silu = gate * sigmoid
    gated = out * silu
    gain = gain_ref[...]
    normed_ref[...] = (gated * inverse_rms * gain).astype(BF16)
    grad_gated = inverse_rms * (gain * cot_ref[...].astype(F32)) - gated * factor
    grad_gate_ref[...] = (
        grad_gated * out * sigmoid * (1.0 + gate * (1.0 - sigmoid))
    ).astype(BF16)
    up = grad_gated * silu
    up_ref[...] = up
    running = running_sums(a_ref[...])
    reached = up * spread(jnp.exp(running), width)
    leaving_ref[...] += jnp.exp(before[:1, :]) * state_terms(reached, c_ref[...])
    end = running[SPAN - 1 :, :]
    before[...] += spread(jnp.broadcast_to(end, (8, end.shape[1])), width)


def diagonal_grad_kernel(
    x_ref, a_ref, b_ref, c_ref, up_ref, grad_x_ref, grad_b_ref, grad_c_ref
):
    heads = a_ref.shape[1]
    size = x_ref.shape[1] // heads
    running = running_sums(a_ref[...])
    running_rows = rows_of(running)
    row, col = iotas(SPAN, SPAN)
    causal = row >= col
    scores = dot(c_ref[...], b_ref[...], 1, 1)
    grad_scores = jnp.zeros((SPAN, SPAN), F32)
    for pair in range(heads // 2):
        cols = slice(pair * 2 * size, (pair + 1) * 2 * size)
        x_pair = x_ref[:, cols]
        high, low = split2(up_ref[:, cols])
        up_cat = jnp.concatenate([high, low], 1)
        left, right = [], []
        for which in range(2):
            decays = decays_of(running, running_rows, 2 * pair + which, causal)
            w_high, w_low = split2(decays * scores)
            x_half = pair_columns(x_pair, which == 0)
            grad_w = dot(up_cat, jnp.concatenate([x_half, x_half], 1), 1, 1)
            grad_scores = grad_scores + decays * grad_w
            u_high = pair_columns(high, which == 0)
            left += [w_high, w_low, w_high]
            right += [u_high, u_high, pair_columns(low, which == 0)]
        grad_x_ref[:, cols] = dot(
            jnp.concatenate(left, 0), jnp.concatenate(right, 0), 0, 0
        )
    g_high, g_low = split2(grad_scores)
    b_half, c_half = b_ref[...], c_ref[...]
    grad_c_ref[...] = dot(
        jnp.concatenate([g_high, g_low], 1), jnp.concatenate([b_half, b_half], 0)
    )
    grad_b_ref[...] = dot(
        jnp.concatenate([g_high, g_low], 0), jnp.concatenate([c_half, c_half], 0), 0, 0
    )


def wide_product(a_parts, b_parts):
    return (
        dot(a_parts[0], b_parts[0], 1, 1)
        + dot(a_parts[1], b_parts[0], 1, 1)
        + dot(a_parts[0], b_parts[1], 1, 1)
    )


def backward_kernel(
    x_ref, a_ref, b_ref, c_ref, up_ref, y_ref, state_ref, diag_ref, gathered_ref,
    leaving_ref, part_b_ref, part_c_ref,
    grad_x_ref, grad_a_ref, grad_b_ref, grad_c_ref, carry,
):
    heads = a_ref.shape[1]
    width = x_ref.shape[1]
    size = b_ref.shape[1]

    @pl.when(pl.program_id(0) == 0)
    def _():
        count = gathered_ref.shape[0]
        place = lax.axis_index("seq")
        adjoint = jnp.zeros((size, width), F32)
        for source in range(count - 1, 0, -1):
            later = jnp.exp(gathered_ref[source, :1, :]) * adjoint
            adjoint = jnp.where(source > place, later + leaving_ref[source], adjoint)
        carry[...] = adjoint

    x = x_ref[...].astype(F32)
    up = up_ref[...]
    b_half, c_half = b_ref[...], c_ref[...]
    running = running_sums(a_ref[...])
    end = running[SPAN - 1 :, :]
    reach = spread(jnp.exp(running), width)
    to_end = spread(jnp.exp(end - running), width)
    end_wide = reach[SPAN - 1 :, :]
    adjoint, state = carry[...], state_ref[...]
    adjoint_parts, state_parts = split2(adjoint), split2(state)
    scaled = x * to_end
    reached = up * reach
    scaled_parts, reached_parts = split2(scaled), split2(reached)
    grad_x = diag_ref[...] + to_end * read_state(b_half, adjoint_parts)
    grad_x_ref[...] = grad_x.astype(BF16)
    grad_c_ref[...] = part_c_ref[...] + wide_product(reached_parts, state_parts)
    grad_b_ref[...] = part_b_ref[...] + wide_product(scaled_parts, adjoint_parts)
    b_twice = jnp.concatenate([b_half, b_half], 0)
    state_end = end_wide * state + dot(b_twice, jnp.concatenate(scaled_parts, 0), 0, 0)
    last = jnp.sum(adjoint * state_end, axis=0, keepdims=True)
    c_twice = jnp.concatenate([c_half, c_half], 0)
    carry[...] = end_wide * adjoint + dot(
        c_twice, jnp.concatenate(reached_parts, 0), 0, 0
    )
    row = lax.broadcasted_iota(jnp.int32, (SPAN, width), 0)
    change = up * y_ref[...] - x * grad_x
    change = change + jnp.where(row == SPAN - 1, last, 0.0)
    grad_running = head_sums(change, heads)
    row, col = iotas(SPAN, SPAN)
    upper = jnp.where(row <= col, 1.0, 0.0).astype(BF16)
    grad_a_ref[...] = dot(
        jnp.concatenate([upper] * 3, 1), jnp.concatenate(split3(grad_running), 0)
    )


def per_device(inputs, gate_input, log_decay, b_matrix, c_matrix, norm_gain, cotangent):
    tokens, width = inputs.shape
    heads = log_decay.shape[1]
    size = b_matrix.shape[2]
    blocks = tokens // SPAN
    seq = lax.axis_size("seq")
    full_width = width * lax.axis_size("head")
    b_half = b_matrix.reshape(tokens, size)
    c_half = c_matrix.reshape(tokens, size)
    gain = norm_gain.reshape(1, width)

    def rows(cols, height=SPAN):
        return pl.BlockSpec((height, cols), lambda k: (k, 0))

    def back(cols):
        return pl.BlockSpec((SPAN, cols), lambda k: (blocks - 1 - k, 0))

    def whole(*shape):
        return pl.BlockSpec(shape, lambda k: (0,) * len(shape))

    def shape(*dims, dtype=F32):
        return jax.ShapeDtypeStruct(dims, dtype)

    def call(kernel, in_specs, out_specs, out_shape, flops, moved, scratch=()):
        return pl.pallas_call(
            kernel,
            grid=(blocks,),
            in_specs=in_specs,
            out_specs=out_specs,
            out_shape=out_shape,
            scratch_shapes=list(scratch),
            compiler_params=pltpu.CompilerParams(
                dimension_semantics=("arbitrary",), vmem_limit_bytes=VMEM_BYTES
            ),
            cost_estimate=pl.CostEstimate(
                flops=flops, bytes_accessed=moved, transcendentals=0
            ),
        )

    mega = 1 << 20
    carry = pltpu.VMEM((size, width), F32)
    local = call(
        local_state_kernel,
        [rows(width), rows(heads), rows(size)],
        whole(size + 8, width),
        shape(size + 8, width),
        600 * mega,
        3 * mega,
    )(inputs, log_decay, b_half)
    gathered = lax.all_gather(local, "seq")
    diagonal = call(
        diagonal_kernel,
        [rows(width), rows(heads), rows(size), rows(size)],
        rows(width),
        shape(tokens, width),
        5000 * mega,
        8 * mega,
    )(inputs, log_decay, b_half, c_half)
    ssd_out, states, sums = call(
        forward_kernel,
        [
            rows(width), rows(width), rows(heads), rows(size), rows(size), rows(width),
            rows(width), whole(1, width), whole(seq, size + 8, width),
        ],
        [rows(width), rows(width, size), rows(SPAN, 8)],
        [shape(tokens, width), shape(blocks * size, width), shape(blocks * 8, SPAN)],
        1500 * mega,
        20 * mega,
        [carry],
    )(diagonal, inputs, log_decay, b_half, c_half, gate_input, cotangent, gain, gathered)
    sums = lax.psum(sums, "head")
    normed, grad_gate, upstream, leaving = call(
        functools.partial(norm_kernel, full_width),
        [
            rows(width), rows(heads), rows(size), rows(width), rows(width),
            whole(1, width), rows(SPAN, 8),
        ],
        [rows(width), rows(width), rows(width), whole(size, width)],
        [
            shape(tokens, width, dtype=BF16), shape(tokens, width, dtype=BF16),
            shape(tokens, width), shape(size, width),
        ],
        1000 * mega,
        20 * mega,
        [pltpu.VMEM((8, width), F32)],
    )(ssd_out, log_decay, c_half, gate_input, cotangent, gain, sums)
    all_leaving = lax.all_gather(leaving, "seq")
    diagonal_grad, part_b, part_c = call(
        diagonal_grad_kernel,
        [rows(width), rows(heads), rows(size), rows(size), rows(width)],
        [rows(width), rows(size), rows(size)],
        [shape(tokens, width), shape(tokens, size), shape(tokens, size)],
        8000 * mega,
        12 * mega,
    )(inputs, log_decay, b_half, c_half, upstream)
    grad_x, grad_a, grad_b, grad_c = call(
        backward_kernel,
        [
            back(width), back(heads), back(size), back(size), back(width), back(width),
            pl.BlockSpec((size, width), lambda k: (blocks - 1 - k, 0)), back(width),
            pl.BlockSpec((seq, 8, width), lambda k: (0, size // 8, 0)),
            whole(seq, size, width), back(size), back(size),
        ],
        [back(width), back(heads), back(size), back(size)],
        [
            shape(tokens, width, dtype=BF16), shape(tokens, heads),
            shape(tokens, size), shape(tokens, size),
        ],
        3000 * mega,
        30 * mega,
        [carry],
    )(
        inputs, log_decay, b_half, c_half, upstream, ssd_out, states, diagonal_grad,
        gathered, all_leaving, part_b, part_c,
    )
    return (
        normed, grad_x, grad_gate, grad_a,
        grad_b.reshape(b_matrix.shape), grad_c.reshape(c_matrix.shape),
    )


def solution(mesh):
    wide = P("seq", "head")
    grouped = P("seq", "head", None)
    return jax.shard_map(
        per_device,
        mesh=mesh,
        in_specs=(wide, wide, wide, grouped, grouped, P("head"), wide),
        out_specs=(wide, wide, wide, wide, grouped, grouped),
        check_vma=False,
    )
```

profile of v0, /device:TPU:0, one launch (start us, length us, event | category | flops | bytes accessed | tf_op | source)
XLA Modules:
  0.0 240.0 jit_solution(2411276078182612911)
XLA Ops:
  7.2 0.0 copy-start.8
  7.2 0.0 copy-start.6
  7.2 0.0 all-gather.5.cloned.1.call-start
  7.2 1.1 copy.13.a_ref
  8.3 0.0 copy-start
  8.3 1.6 copy-done
  9.9 0.0 copy-start.7
  9.9 0.9 copy-done.7
  10.9 6.9 %shard_map.119 = f32[136,1024]{1,0:T(8,128)} custom-call(bf16[1024,1024]{1,0:T(8,128)(2,1)S(1)} %copy-done, f32[1024,16]{1,0:T(8,128)S(1)} %copy.13.a_ref, bf16[1024,128]{1,0:T(8,128)(2,1)S(1)} %bitcast.16), custom_call_target="tpu_custom_call" | custom-call | flops 629145600 | bytes 3145728 | tf_op jit(solution)/shard_map/pallas_call | solution.py:369
  17.8 0.0 all-gather.5.cloned.1.call-update
  17.8 0.0 all-gather.7.cloned.1.call-start
  17.8 0.0 copy-done.8
  17.8 0.0 copy-done.6
  17.9 0.0 copy-start.1
  17.9 1.6 copy-done.1
  19.5 0.0 copy-start.2
  19.5 0.0 copy-start.15
  19.5 7.1 %shard_map.118.diag_ref = f32[1024,1024]{1,0:T(8,128)} custom-call(bf16[1024,1024]{1,0:T(8,128)(2,1)S(1)} %copy-done.1, f32[1024,16]{1,0:T(8,128)S(1)} %copy.13.a_ref, bf16[1024,128]{1,0:T(8,128)(2,1)S(1)} %bitcast.17, bf16[1024,128]{1,0:T(8,128)(2,1)S(1)} %bitcast.11), custom_call_target="tpu_custom_call" | custom-call | flops 5242880000 | bytes 8388608 | tf_op jit(solution)/shard_map/pallas_call | solution.py:378
  26.6 70.7 %all-gather.5.cloned.1.call-done = f32[1088,1024]{1,0:T(8,128)} async-done(((f32[136,1024]{1,0:T(8,128)}), f32[1088,1024]{1,0:T(8,128)}) %all-gather.5.cloned.1.call-update) | async-done | bytes 4456464 | tf_op jit(solution)/shard_map/all_gather | solution.py:377
  97.3 0.0 copy-done.2
  97.3 0.0 copy-done.15
  97.3 0.0 copy-start.3
  97.3 1.6 copy-done.3
  98.9 12.3 %shard_map.120 = (f32[1024,1024]{1,0:T(8,128)}, f32[1024,1024]{1,0:T(8,128)}, f32[64,128]{1,0:T(8,128)S(1)}) custom-call(f32[1024,1024]{1,0:T(8,128)} %shard_map.118.diag_ref, bf16[1024,1024]{1,0:T(8,128)(2,1)S(1)} %copy-done.2, f32[1024,16]{1,0:T(8,128)S(1)} %copy.13.a_ref, bf16[1024,128]{1,0:T(8,128)(2,1)S(1)} %bitcast.18, bf16[1024,128]{1,0:T(8,128)(2,1)S(1)} %bitcast.12, ...), custom_call_target="tpu_custom_call" | custom-call | flops 1572864000 | bytes 20971520 | tf_op jit(solution)/shard_map/pallas_call | solution.py:386
  111.2 10.3 %psum.7.sums_ref = f32[64,128]{1,0:T(8,128)S(1)} all-reduce(f32[64,128]{1,0:T(8,128)S(1)} %get-tuple-element.21), channel_id=1, replica_groups=mesh['seq'=8,'head'=4] {'head'}, use_global_device_ids=true, to_apply=%region_0.0 | all-reduce | flops 8192 | bytes 65536 | tf_op jit(solution)/shard_map/psum | solution.py:398
  121.5 0.0 copy-start.4
  121.5 1.6 copy-done.4
  123.1 0.0 copy-start.5
  123.1 1.6 copy-done.5
  124.6 10.6 %shard_map.121 = (bf16[1024,1024]{1,0:T(8,128)(2,1)}, bf16[1024,1024]{1,0:T(8,128)(2,1)}, f32[1024,1024]{1,0:T(8,128)}, f32[128,1024]{1,0:T(8,128)S(1)}) custom-call(f32[1024,1024]{1,0:T(8,128)} %get-tuple-element.20.y_ref, f32[1024,16]{1,0:T(8,128)S(1)} %copy.13.a_ref, bf16[1024,128]{1,0:T(8,128)(2,1)S(1)} %bitcast.13, bf16[1024,1024]{1,0:T(8,128)(2,1)S(1)} %copy-done.4, ...), custom_call_target="tpu_custom_call" | custom-call | flops 1048576000 | bytes 20971520 | tf_op jit(solution)/shard_map/pallas_call | solution.py:399
  135.2 0.0 copy-start.14
  135.2 0.8 copy-done.14
  136.0 0.0 all-gather.7.cloned.1.call-update
  136.0 14.8 %shard_map.122 = (f32[1024,1024]{1,0:T(8,128)}, f32[1024,128]{1,0:T(8,128)S(1)}, f32[1024,128]{1,0:T(8,128)S(1)}) custom-call(bf16[1024,1024]{1,0:T(8,128)(2,1)S(1)} %copy-done.2, f32[1024,16]{1,0:T(8,128)S(1)} %copy.13.a_ref, bf16[1024,128]{1,0:T(8,128)(2,1)S(1)} %bitcast.19, bf16[1024,128]{1,0:T(8,128)(2,1)S(1)} %bitcast.14, ...), custom_call_target="tpu_custom_call" | custom-call | flops 8388608000 | bytes 12582912 | tf_op jit(solution)/shard_map/pallas_call | solution.py:415
  150.8 0.0 copy-start.9
  150.8 0.8 copy-done.9
  151.6 0.0 copy-start.11
  151.6 0.8 copy-done.11
  152.4 55.5 %all-gather.7.cloned.1.call-done = f32[1024,1024]{1,0:T(8,128)} async-done(((f32[128,1024]{1,0:T(8,128)}), f32[1024,1024]{1,0:T(8,128)}) %all-gather.7.cloned.1.call-update) | async-done | bytes 4194320 | tf_op jit(solution)/shard_map/all_gather | solution.py:414
  207.9 0.0 copy-start.10
  207.9 1.0 copy-done.10
  209.0 0.0 copy-start.12
  209.0 1.0 copy-done.12
  210.0 20.5 %shard_map.123 = (bf16[1024,1024]{1,0:T(8,128)(2,1)}, f32[1024,16]{1,0:T(8,128)S(1)}, f32[1024,128]{1,0:T(8,128)}, f32[1024,128]{1,0:T(8,128)}) custom-call(bf16[1024,1024]{1,0:T(8,128)(2,1)S(1)} %copy-done.2, f32[1024,16]{1,0:T(8,128)S(1)} %copy.13.a_ref, bf16[1024,128]{1,0:T(8,128)(2,1)S(1)} %bitcast.20, bf16[1024,128]{1,0:T(8,128)(2,1)S(1)} %bitcast.15, ...), custom_call_target="tpu_custom_call" | custom-call | flops 3145728000 | bytes 31457280 | tf_op jit(solution)/shard_map/pallas_call | solution.py:423
  230.5 0.0 copy-start.13
  230.5 0.8 copy-done.13
  231.3 1.8 copy.19
Async XLA Ops:
  7.2 10.7 %copy-start.8 = (bf16[1024,1,128]{2,0,1:T(8,128)(2,1)S(1)}, bf16[1024,1,128]{2,0,1:T(8,128)(2,1)}, u32[]{:S(2)}) copy-start(bf16[1024,1,128]{2,0,1:T(8,128)(2,1)} %param.10) | copy-start | bytes 786436
  7.2 10.7 %copy-start.6 = (bf16[1024,1,128]{2,0,1:T(8,128)(2,1)S(1)}, bf16[1024,1,128]{2,0,1:T(8,128)(2,1)}, u32[]{:S(2)}) copy-start(bf16[1024,1,128]{2,0,1:T(8,128)(2,1)} %param.11) | copy-start | bytes 786436
  7.2 90.1 %all-gather.5.cloned.1.call-start = ((), (), s32[]{:S(2)}) async-start(), calls=%async_computation | async-start | bytes 5013504 | tf_op jit(solution)/shard_map/all_gather | solution.py:377
  8.3 1.6 copy-start
  9.9 0.9 copy-start.7
  17.8 190.1 %all-gather.7.cloned.1.call-start = ((), (), s32[]{:S(2)}) async-start(), calls=%async_computation.1 | async-start | bytes 4718592 | tf_op jit(solution)/shard_map/all_gather | solution.py:414
  17.9 1.6 copy-start.1
  19.5 77.8 %copy-start.2 = (bf16[1024,1024]{1,0:T(8,128)(2,1)S(1)}, bf16[1024,1024]{1,0:T(8,128)(2,1)}, u32[]{:S(2)}) copy-start(bf16[1024,1024]{1,0:T(8,128)(2,1)} %x_ref.9) | copy-start | bytes 6291460
  19.5 77.8 %copy-start.15 = (f32[1024]{0:T(1024)S(1)}, f32[1024]{0:T(1024)}, u32[]{:S(2)}) copy-start(f32[1024]{0:T(1024)} %param.12) | copy-start | bytes 12292
  97.3 1.6 copy-start.3
  121.5 1.6 copy-start.4
  123.1 1.6 copy-start.5
  135.2 0.8 copy-start.14
  150.8 0.8 copy-start.9
  151.6 0.8 copy-start.11
  207.9 1.0 copy-start.10
  209.0 1.0 copy-start.12
  230.5 0.8 copy-start.13
Sparse Core Ops, SparseCore 0:
  17.9 79.3 all-gather.4
  136.2 71.7 all-gather.6
where the time goes:
time: 241 us; the launch traced here: 240 us
  waiting for transfers between devices  126 us (52%)
  Pallas kernels  72.2 us (30%)
  local copies, waits for them, and re-layouts  17.1 us (7%)
  between operations  14.1 us (6%)
  blocking collectives  10.3 us (4%)
    all_gather x1, waiting for transfers between devices, per_device(): gathered = lax.all_gather(local, 'seq')  70.7 us
    all_gather x1, waiting for transfers between devices, per_device(): all_leaving = lax.all_gather(leaving, 'seq')  55.5 us
    pallas_call x1, Pallas kernels, per_device(): call(backward_kernel, [back(width), back(heads), back(size), back(size),...  20.5 us
    unnamed x34, local copies, waits for them, and re-layouts  17.1 us
    pallas_call x1, Pallas kernels, per_device(): call(diagonal_grad_kernel, [rows(width), rows(heads), rows(size), rows(si...  14.8 us
    pallas_call x1, Pallas kernels, per_device(): call(forward_kernel, [rows(width), rows(width), rows(heads), rows(size),...  12.3 us
    pallas_call x1, Pallas kernels, per_device(): call(functools.partial(norm_kernel, full_width), [rows(width), rows(heads...  10.6 us
    psum x1, blocking collectives, per_device(): sums = lax.psum(sums, 'head')  10.3 us
  transfers between devices with their start and end apart: 2, of which 2 were waited for; matrix products, arithmetic and copies ran while one was open for 0% of the time, Pallas kernels for 9%

commit v1 on v0

--- a/solution.py
+++ b/solution.py
@@ -11,7 +11,7 @@
 EPSILON = 1e-05
 F32 = jnp.float32
 BF16 = jnp.bfloat16
-VMEM_BYTES = 48 * 1024 * 1024
+VMEM_BYTES = 60 * 1024 * 1024
 
 
 def split2(v):
@@ -49,14 +49,14 @@
     return jnp.where((row >= col * size) & (row < (col + 1) * size), 1.0, 0.0).astype(BF16)
 
 
-def spread(v, width):
+def spread(v, width, parts=split2):
     matrix = spread_matrix(v.shape[1], width)
-    return sum(dot(p, matrix) for p in split3(v))
+    return sum(dot(p, matrix) for p in parts(v))
 
 
 def head_sums(v, heads):
     matrix = gather_matrix(heads, v.shape[1])
-    return sum(dot(p, matrix) for p in split3(v))
+    return sum(dot(p, matrix) for p in split2(v))
 
 
 def running_sums(a):
@@ -75,22 +75,22 @@
     return dot(jnp.concatenate([matrix_half] * 2, 1), jnp.concatenate(state_parts, 0))
 
 
-def local_state_kernel(x_ref, a_ref, b_ref, out_ref):
+def local_state_kernel(x_ref, a_ref, b_ref, out_ref, total_ref):
     width = x_ref.shape[1]
-    size = b_ref.shape[1]
 
     @pl.when(pl.program_id(0) == 0)
     def _():
         out_ref[...] = jnp.zeros_like(out_ref)
+        total_ref[...] = jnp.zeros_like(total_ref)
 
     running = running_sums(a_ref[...])
     end = running[SPAN - 1 :, :]
     scaled = x_ref[...].astype(F32) * spread(jnp.exp(end - running), width)
-    end_wide = spread(jnp.broadcast_to(end, (8, end.shape[1])), width)
-    out_ref[:size, :] = out_ref[:size, :] * jnp.exp(end_wide[:1, :]) + state_terms(
+    end_wide = spread(jnp.broadcast_to(end, (8, end.shape[1])), width, split3)
+    out_ref[...] = out_ref[...] * jnp.exp(end_wide[:1, :]) + state_terms(
         scaled, b_ref[...]
     )
-    out_ref[size:, :] += end_wide
+    total_ref[...] += end_wide
 
 
 def pair_columns(pair_x, first):
@@ -130,16 +130,87 @@
         y_ref[:, cols] = dot(jnp.concatenate(left, 1), jnp.concatenate(right, 0))
 
 
-def carried(gathered_ref, size, reverse):
-    count = gathered_ref.shape[0]
+def chain_kernel(
+    reverse, own_ref, total_ref, out_ref, landed, onward, send_sem, recv_sem
+):
+    count = lax.axis_size("seq")
     place = lax.axis_index("seq")
-    state = jnp.zeros((size, gathered_ref.shape[2]), F32)
-    for hop in range(count - 1):
-        source = count - 1 - hop if reverse else hop
-        use = source > place if reverse else source < place
-        later = jnp.exp(gathered_ref[source, size : size + 1, :]) * state
-        state = jnp.where(use, later + gathered_ref[source, :size, :], state)
-    return state
+    up, down = lax.rem(place + 1, count), lax.rem(place + count - 1, count)
+    first, last = place == 0, place == count - 1
+    target, source = (down, up) if reverse else (up, down)
+    starts, ends = (last, first) if reverse else (first, last)
+    column = lax.axis_index("head")
+    barrier = pltpu.get_barrier_semaphore()
+    pl.semaphore_signal(
+        barrier, inc=1, device_id=(source, column), device_id_type=pl.DeviceIdType.MESH
+    )
+    pl.semaphore_wait(barrier, 1)
+    chunks = out_ref.shape[0] // 8
+
+    def chunk(i):
+        return pl.ds(pl.multiple_of(i * 8, 8), 8)
+
+    def copy(i):
+        return pltpu.make_async_remote_copy(
+            src_ref=onward.at[chunk(i)],
+            dst_ref=landed.at[chunk(i)],
+            send_sem=send_sem.at[i],
+            recv_sem=recv_sem.at[i],
+            device_id=(target, column),
+            device_id_type=pl.DeviceIdType.MESH,
+        )
+
+    @pl.when(starts)
+    def _():
+        out_ref[...] = jnp.zeros_like(out_ref)
+
+    def step(i, nothing):
+        @pl.when(jnp.logical_not(starts))
+        def _():
+            copy(i).wait_recv()
+            out_ref[chunk(i), :] = landed[chunk(i), :]
+
+        @pl.when(jnp.logical_not(ends))
+        def _():
+            decay = jnp.exp(total_ref[0:1, :])
+            onward[chunk(i), :] = decay * out_ref[chunk(i), :] + own_ref[chunk(i), :]
+            copy(i).start()
+
+        return nothing
+
+    lax.fori_loop(0, chunks, step, 0)
+
+    @pl.when(jnp.logical_not(ends))
+    def _():
+        def finish(i, nothing):
+            copy(i).wait_send()
+            return nothing
+
+        lax.fori_loop(0, chunks, finish, 0)
+
+
+def chain(own, totals, reverse):
+    rows, width = own.shape
+    return pl.pallas_call(
+        functools.partial(chain_kernel, reverse),
+        out_shape=jax.ShapeDtypeStruct((rows, width), F32),
+        in_specs=[pl.BlockSpec(memory_space=pltpu.VMEM)] * 2,
+        out_specs=pl.BlockSpec(memory_space=pltpu.VMEM),
+        scratch_shapes=[
+            pltpu.VMEM((rows, width), F32),
+            pltpu.VMEM((rows, width), F32),
+            pltpu.SemaphoreType.DMA((rows // 8,)),
+            pltpu.SemaphoreType.DMA((rows // 8,)),
+        ],
+        compiler_params=pltpu.CompilerParams(
+            collective_id=1 if reverse else 0,
+            has_side_effects=True,
+            vmem_limit_bytes=VMEM_BYTES,
+        ),
+        cost_estimate=pl.CostEstimate(
+            flops=1 << 20, bytes_accessed=4 << 20, transcendentals=0
+        ),
+    )(own, totals)
 
 
 def silu_parts(gate_ref):
@@ -156,15 +227,14 @@
 
 
 def forward_kernel(
-    diag_ref, x_ref, a_ref, b_ref, c_ref, gate_ref, cot_ref, gain_ref, gathered_ref,
+    diag_ref, x_ref, a_ref, b_ref, c_ref, gate_ref, cot_ref, gain_ref, incoming_ref,
     y_ref, state_ref, sums_ref, carry,
 ):
     width = x_ref.shape[1]
-    size = b_ref.shape[1]
 
     @pl.when(pl.program_id(0) == 0)
     def _():
-        carry[...] = carried(gathered_ref, size, False)
+        carry[...] = incoming_ref[...]
 
     running = running_sums(a_ref[...])
     end = running[SPAN - 1 :, :]
@@ -221,7 +291,7 @@
     reached = up * spread(jnp.exp(running), width)
     leaving_ref[...] += jnp.exp(before[:1, :]) * state_terms(reached, c_ref[...])
     end = running[SPAN - 1 :, :]
-    before[...] += spread(jnp.broadcast_to(end, (8, end.shape[1])), width)
+    before[...] += spread(jnp.broadcast_to(end, (8, end.shape[1])), width, split3)
 
 
 def diagonal_grad_kernel(
@@ -272,23 +342,16 @@
 
 
 def backward_kernel(
-    x_ref, a_ref, b_ref, c_ref, up_ref, y_ref, state_ref, diag_ref, gathered_ref,
-    leaving_ref, part_b_ref, part_c_ref,
+    x_ref, a_ref, b_ref, c_ref, up_ref, y_ref, state_ref, diag_ref, incoming_ref,
+    part_b_ref, part_c_ref,
     grad_x_ref, grad_a_ref, grad_b_ref, grad_c_ref, carry,
 ):
     heads = a_ref.shape[1]
     width = x_ref.shape[1]
-    size = b_ref.shape[1]
 
     @pl.when(pl.program_id(0) == 0)
     def _():
-        count = gathered_ref.shape[0]
-        place = lax.axis_index("seq")
-        adjoint = jnp.zeros((size, width), F32)
-        for source in range(count - 1, 0, -1):
-            later = jnp.exp(gathered_ref[source, :1, :]) * adjoint
-            adjoint = jnp.where(source > place, later + leaving_ref[source], adjoint)
-        carry[...] = adjoint
+        carry[...] = incoming_ref[...]
 
     x = x_ref[...].astype(F32)
     up = up_ref[...]
@@ -330,7 +393,6 @@
     heads = log_decay.shape[1]
     size = b_matrix.shape[2]
     blocks = tokens // SPAN
-    seq = lax.axis_size("seq")
     full_width = width * lax.axis_size("head")
     b_half = b_matrix.reshape(tokens, size)
     c_half = c_matrix.reshape(tokens, size)
@@ -366,15 +428,15 @@
 
     mega = 1 << 20
     carry = pltpu.VMEM((size, width), F32)
-    local = call(
+    local, totals = call(
         local_state_kernel,
         [rows(width), rows(heads), rows(size)],
-        whole(size + 8, width),
-        shape(size + 8, width),
+        [whole(size, width), whole(8, width)],
+        [shape(size, width), shape(8, width)],
         600 * mega,
         3 * mega,
     )(inputs, log_decay, b_half)
-    gathered = lax.all_gather(local, "seq")
+    incoming = chain(local, totals, False)
     diagonal = call(
         diagonal_kernel,
         [rows(width), rows(heads), rows(size), rows(size)],
@@ -387,14 +449,14 @@
         forward_kernel,
         [
             rows(width), rows(width), rows(heads), rows(size), rows(size), rows(width),
-            rows(width), whole(1, width), whole(seq, size + 8, width),
+            rows(width), whole(1, width), whole(size, width),
         ],
         [rows(width), rows(width, size), rows(SPAN, 8)],
         [shape(tokens, width), shape(blocks * size, width), shape(blocks * 8, SPAN)],
         1500 * mega,
         20 * mega,
         [carry],
-    )(diagonal, inputs, log_decay, b_half, c_half, gate_input, cotangent, gain, gathered)
+    )(diagonal, inputs, log_decay, b_half, c_half, gate_input, cotangent, gain, incoming)
     sums = lax.psum(sums, "head")
     normed, grad_gate, upstream, leaving = call(
         functools.partial(norm_kernel, full_width),
@@ -411,7 +473,7 @@
         20 * mega,
         [pltpu.VMEM((8, width), F32)],
     )(ssd_out, log_decay, c_half, gate_input, cotangent, gain, sums)
-    all_leaving = lax.all_gather(leaving, "seq")
+    adjoint = chain(leaving, totals, True)
     diagonal_grad, part_b, part_c = call(
         diagonal_grad_kernel,
         [rows(width), rows(heads), rows(size), rows(size), rows(width)],
@@ -425,8 +487,7 @@
         [
             back(width), back(heads), back(size), back(size), back(width), back(width),
             pl.BlockSpec((size, width), lambda k: (blocks - 1 - k, 0)), back(width),
-            pl.BlockSpec((seq, 8, width), lambda k: (0, size // 8, 0)),
-            whole(seq, size, width), back(size), back(size),
+            whole(size, width), back(size), back(size),
         ],
         [back(width), back(heads), back(size), back(size)],
         [
@@ -438,7 +499,7 @@
         [carry],
     )(
         inputs, log_decay, b_half, c_half, upstream, ssd_out, states, diagonal_grad,
-        gathered, all_leaving, part_b, part_c,
+        adjoint, part_b, part_c,
     )
     return (
         normed, grad_x, grad_gate, grad_a,

time: 241 us -> 162 us (0.67)
  waiting for transfers between devices: 126 us -> 0 us
  Pallas kernels: 72.2 us -> 145 us
  between operations: 14.1 us -> 0.66 us
  local copies, waits for them, and re-layouts: 17.1 us -> 3.68 us
    all_gather x2 -> x0, waiting for transfers between devices: 126 us -> none  [the longest x1 70.7 us: per_device(): gathered = lax.all_gather(local, 'seq')]
    pallas_call x1 -> x3, Pallas kernels: 6.89 us -> 79.2 us  [the longest x2 70.9 us: chain(): pl.pallas_call(functools.partial(chain_kernel, reverse), out_shape=jax.Sh...]
    unnamed x34 -> x2, local copies, waits for them, and re-layouts: 17.1 us -> 3.68 us
  transfers between devices with their start and end apart: 2 -> 0, of which waited for: 2 -> 0; matrix products, arithmetic and copies ran while one was open for 0% -> 0% of each run, Pallas kernels for 9% -> 0%
where the time goes in v1:
time: 162 us; the launch traced here: 161 us
  Pallas kernels  145 us (90%)
  blocking collectives  11.4 us (7%)
  local copies, waits for them, and re-layouts  3.68 us (2%)
    pallas_call x2, Pallas kernels, chain(): pl.pallas_call(functools.partial(chain_kernel, reverse), out_shape=jax.Sh...  70.9 us
    pallas_call x1, Pallas kernels, per_device(): call(backward_kernel, [back(width), back(heads), back(size), back(size),...  18.3 us
    pallas_call x1, Pallas kernels, per_device(): call(diagonal_grad_kernel, [rows(width), rows(heads), rows(size), rows(si...  15.1 us
    pallas_call x1, Pallas kernels, per_device(): call(forward_kernel, [rows(width), rows(width), rows(heads), rows(size),...  11.8 us
    psum x1, blocking collectives, per_device(): sums = lax.psum(sums, 'head')  11.4 us
    pallas_call x1, Pallas kernels, per_device(): call(functools.partial(norm_kernel, full_width), [rows(width), rows(heads...  11.4 us
    pallas_call x1, Pallas kernels, per_device(): call(diagonal_kernel, [rows(width), rows(heads), rows(size), rows(size)],...  9.42 us
    pallas_call x1, Pallas kernels, per_device(): call(local_state_kernel, [rows(width), rows(heads), rows(size)], [whole(s...  8.35 us

profile of v1, /device:TPU:0, one launch (start us, length us, event | category | flops | bytes accessed | tf_op | source)
XLA Modules:
  0.0 161.0 jit_solution(10936360262150633433)
XLA Ops:
  0.6 1.8 %copy.13.a_ref = f32[1024,16]{1,0:T(8,128)} copy(f32[1024,16]{0,1:T(8,128)} %param.9) | data formatting | bytes 131072 | tf_op args[2]
  2.5 8.4 %shard_map.119 = (f32[128,1024]{1,0:T(8,128)}, f32[8,1024]{1,0:T(8,128)}) custom-call(bf16[1024,1024]{1,0:T(8,128)(2,1)} %x_ref.9, f32[1024,16]{1,0:T(8,128)} %copy.13.a_ref, bf16[1024,128]{1,0:T(8,128)(2,1)} %bitcast.14), custom_call_target="tpu_custom_call" | custom-call | flops 629145600 | bytes 3145728 | tf_op jit(solution)/shard_map/pallas_call | solution.py:431
  10.8 16.3 %shard_map.120.incoming_ref = f32[128,1024]{1,0:T(8,128)} custom-call(f32[128,1024]{1,0:T(8,128)} %get-tuple-element.22.own_ref, f32[8,1024]{1,0:T(8,128)} %get-tuple-element.23.total_ref), custom_call_target="tpu_custom_call" | custom-call | flops 1048576 | bytes 4194304 | tf_op jit(solution)/shard_map/pallas_call | solution.py:194
  27.1 9.4 %shard_map.118.diag_ref = f32[1024,1024]{1,0:T(8,128)} custom-call(bf16[1024,1024]{1,0:T(8,128)(2,1)} %x_ref.9, f32[1024,16]{1,0:T(8,128)} %copy.13.a_ref, bf16[1024,128]{1,0:T(8,128)(2,1)} %bitcast.15, bf16[1024,128]{1,0:T(8,128)(2,1)} %bitcast.9), custom_call_target="tpu_custom_call" | custom-call | flops 5242880000 | bytes 8388608 | tf_op jit(solution)/shard_map/pallas_call | solution.py:440
  36.6 11.8 %shard_map.121 = (f32[1024,1024]{1,0:T(8,128)}, f32[1024,1024]{1,0:T(8,128)}, f32[64,128]{1,0:T(8,128)}) custom-call(f32[1024,1024]{1,0:T(8,128)} %shard_map.118.diag_ref, bf16[1024,1024]{1,0:T(8,128)(2,1)} %x_ref.9, f32[1024,16]{1,0:T(8,128)} %copy.13.a_ref, bf16[1024,128]{1,0:T(8,128)(2,1)} %bitcast.16, bf16[1024,128]{1,0:T(8,128)(2,1)} %bitcast.10, ...), custom_call_target="tpu_custom_call" | custom-call | flops 1572864000 | bytes 20971520 | tf_op jit(solution)/shard_map/pallas_call | solution.py:448
  48.3 11.4 %psum.7.sums_ref = f32[64,128]{1,0:T(8,128)} all-reduce(f32[64,128]{1,0:T(8,128)} %get-tuple-element.25), channel_id=1, replica_groups=mesh['seq'=8,'head'=4] {'head'}, use_global_device_ids=true, to_apply=%region_0.0 | all-reduce | flops 8192 | bytes 65536 | tf_op jit(solution)/shard_map/psum | solution.py:460
  59.8 11.4 %shard_map.122 = (bf16[1024,1024]{1,0:T(8,128)(2,1)}, bf16[1024,1024]{1,0:T(8,128)(2,1)}, f32[1024,1024]{1,0:T(8,128)}, f32[128,1024]{1,0:T(8,128)}) custom-call(f32[1024,1024]{1,0:T(8,128)} %get-tuple-element.24.y_ref, f32[1024,16]{1,0:T(8,128)} %copy.13.a_ref, bf16[1024,128]{1,0:T(8,128)(2,1)} %bitcast.11, bf16[1024,1024]{1,0:T(8,128)(2,1)} %gate_ref.3, ...), custom_call_target="tpu_custom_call" | custom-call | flops 1048576000 | bytes 20971520 | tf_op jit(solution)/shard_map/pallas_call | solution.py:461
  71.2 54.6 %shard_map.124.incoming_ref = f32[128,1024]{1,0:T(8,128)} custom-call(f32[128,1024]{1,0:T(8,128)} %get-tuple-element.30.own_ref, f32[8,1024]{1,0:T(8,128)} %get-tuple-element.23.total_ref), custom_call_target="tpu_custom_call" | custom-call | flops 1048576 | bytes 4194304 | tf_op jit(solution)/shard_map/pallas_call | solution.py:194
  125.7 15.1 %shard_map.123 = (f32[1024,1024]{1,0:T(8,128)}, f32[1024,128]{1,0:T(8,128)}, f32[1024,128]{1,0:T(8,128)}) custom-call(bf16[1024,1024]{1,0:T(8,128)(2,1)} %x_ref.9, f32[1024,16]{1,0:T(8,128)} %copy.13.a_ref, bf16[1024,128]{1,0:T(8,128)(2,1)} %bitcast.17, bf16[1024,128]{1,0:T(8,128)(2,1)} %bitcast.12, f32[1024,1024]{1,0:T(8,128)} %get-tuple-element.27.up_ref), custom_call_target="tpu_custom_call" | custom-call | flops 8388608000 | bytes 12582912 | tf_op jit(solution)/shard_map/pallas_call | solution.py:477
  140.9 18.3 %shard_map.125 = (bf16[1024,1024]{1,0:T(8,128)(2,1)}, f32[1024,16]{1,0:T(8,128)}, f32[1024,128]{1,0:T(8,128)}, f32[1024,128]{1,0:T(8,128)}) custom-call(bf16[1024,1024]{1,0:T(8,128)(2,1)} %x_ref.9, f32[1024,16]{1,0:T(8,128)} %copy.13.a_ref, bf16[1024,128]{1,0:T(8,128)(2,1)} %bitcast.18, bf16[1024,128]{1,0:T(8,128)(2,1)} %bitcast.13, ...), custom_call_target="tpu_custom_call" | custom-call | flops 3145728000 | bytes 31457280 | tf_op jit(solution)/shard_map/pallas_call | solution.py:485
  159.2 1.8 %copy.19 = f32[1024,16]{0,1:T(8,128)} copy(f32[1024,16]{1,0:T(8,128)} %get-tuple-element.41) | data formatting | bytes 131072
